TPU v7x, 32 devices: a whole 2x2x4 slice. The times are simulated.
32 devices in a mesh: seq: 16 (over z, x, core), blk: 2 (over y).
Axes of the slice: x: 2, y: 2, z: 4, core: 2. Of those that a mesh axis runs over, the one named last changes fastest.
Arguments:
- query_states: bfloat16 [4096, 2048], P(('seq', 'blk')), may hold values from -6 to 6
- key_states: bfloat16 [4096, 2048], P(('seq', 'blk')), may hold values from -6 to 6
- value_states: bfloat16 [4096, 2048], P(('seq', 'blk')), may hold values from -6 to 6
- output_grad: bfloat16 [4096, 2048], P(('seq', 'blk')), may hold values from -6 to 6
- near_mask: int32 [32, 2], replicated, may hold values 0 or 1
- motion_count: int32 [32], replicated, may hold values from 0 to 3
Outputs:
- query_grad: bfloat16 [4096, 2048], P(('seq', 'blk'))
- key_grad: bfloat16 [4096, 2048], P(('seq', 'blk'))
- value_grad: bfloat16 [4096, 2048], P(('seq', 'blk'))
All inputs are finite; a program needn't handle non-finite values.
Results may differ from a plain program's by a relative error of at most 0.012.
Values may be sent and summed in bfloat16 or wider, within the bound.
A program may use at most 64 MiB of HBM per device.

v0:
```python
import jax
import jax.numpy as jnp
from jax import lax
from jax.sharding import PartitionSpec as P

HEAD_DIM = 64
TILE = 128
REACH = 2


def from_behind(block, axis, distance):
    devices = range(lax.axis_size(axis))
    route = [(i - distance, i) for i in devices if i - distance in devices]
    return lax.ppermute(block, axis, route)


def tile_allow(
    mask_rows, motion_rows, query_tile0, key_tile0, tiles_all, query_tiles, key_tiles, tile_size
):
    query_ids = query_tile0 + jnp.arange(query_tiles, dtype=jnp.int32)[:, None]
    key_ids = key_tile0 + jnp.arange(key_tiles, dtype=jnp.int32)[None, :]
    spread = key_ids - query_ids
    near = (
        (spread == 0)
        | (spread == -1) & (mask_rows[:, 0:1] == 1)
        | (spread == 1) & (mask_rows[:, 1:2] == 1)
    )
    far_ok = (jnp.abs(spread) >= 2) & (jnp.abs(spread) <= REACH) & (motion_rows[:, None] >= 2)
    inside = (key_ids >= 0) & (key_ids < tiles_all)
    tile_ok = (near | far_ok) & inside
    spread_out = jnp.broadcast_to(
        tile_ok[:, None, :, None], (query_tiles, tile_size, key_tiles, tile_size)
    )
    return spread_out.reshape(query_tiles * tile_size, key_tiles * tile_size)


def block_grad(query_rows, key_rows, value_rows, grad_rows, allowed, scale_factor):
    scores = jnp.dot(query_rows, key_rows.T, preferred_element_type=jnp.float32) * scale_factor
    scores = jnp.where(allowed, scores, -1e30)
    row_max = jnp.max(scores, axis=1, keepdims=True)
    weights_raw = jnp.exp(scores - row_max)
    probs = weights_raw / jnp.sum(weights_raw, axis=1, keepdims=True)
    probs_b = probs.astype(jnp.bfloat16)
    attn_out = jnp.dot(probs_b, value_rows, preferred_element_type=jnp.float32)
    delta = jnp.sum(grad_rows.astype(jnp.float32) * attn_out, axis=1, keepdims=True)
    dprobs = jnp.dot(grad_rows, value_rows.T, preferred_element_type=jnp.float32)
    dscores = (probs * (dprobs - delta)).astype(jnp.bfloat16)
    query_part = jnp.dot(dscores, key_rows, preferred_element_type=jnp.float32) * scale_factor
    key_part = jnp.dot(dscores.T, query_rows, preferred_element_type=jnp.float32) * scale_factor
    value_part = jnp.dot(probs_b.T, grad_rows, preferred_element_type=jnp.float32)
    return (query_part, key_part, value_part)


def heads_first(matrix, head_count, head_width):
    return matrix.reshape(matrix.shape[0], head_count, head_width).transpose(1, 0, 2)


def heads_last(stacked):
    return stacked.transpose(1, 0, 2).reshape(stacked.shape[1], stacked.shape[0] * stacked.shape[2])


def per_device(query_states, key_states, value_states, output_grad, near_mask, motion_count):
    queries, keys_local, values_local, grads_in = (
        lax.all_to_all(query_states, "blk", split_axis=1, concat_axis=0, tiled=True),
        lax.all_to_all(key_states, "blk", split_axis=1, concat_axis=0, tiled=True),
        lax.all_to_all(value_states, "blk", split_axis=1, concat_axis=0, tiled=True),
        lax.all_to_all(output_grad, "blk", split_axis=1, concat_axis=0, tiled=True),
    )
    group, feats = queries.shape
    head_width = HEAD_DIM
    heads_here = feats // head_width
    rim_rows = REACH * TILE
    paired = jnp.stack([keys_local, values_local])
    from_left = from_behind(paired, "seq", 1)
    from_right = from_behind(paired, "seq", -1)
    padded = jnp.concatenate([from_left, paired, from_right], axis=1)
    padded_len = padded.shape[1]
    block_rows = min(512, group)
    window_rows = block_rows + 2 * rim_rows
    tiles_all = near_mask.shape[0]
    first_tile = lax.axis_index("seq") * (group // TILE)
    scale_factor = float(head_width) ** (-0.5)

    def one_head(per_head):
        head_queries, head_grads, head_keys, head_values = per_head

        def block_step(block_index, running):
            query_all, acc_keys, acc_values = running
            row_start = block_index * block_rows
            key_start = group - rim_rows + row_start
            query_rows = lax.dynamic_slice_in_dim(head_queries, row_start, block_rows, 0)
            grad_rows = lax.dynamic_slice_in_dim(head_grads, row_start, block_rows, 0)
            key_rows = lax.dynamic_slice_in_dim(head_keys, key_start, window_rows, 0)
            value_rows = lax.dynamic_slice_in_dim(head_values, key_start, window_rows, 0)
            query_tile0 = first_tile + row_start // TILE
            mask_rows = lax.dynamic_slice_in_dim(near_mask, query_tile0, block_rows // TILE, 0)
            motion_rows = lax.dynamic_slice_in_dim(motion_count, query_tile0, block_rows // TILE, 0)
            allowed = tile_allow(
                mask_rows,
                motion_rows,
                query_tile0,
                query_tile0 - REACH,
                tiles_all,
                block_rows // TILE,
                window_rows // TILE,
                TILE,
            )
            query_part, key_part, value_part = block_grad(
                query_rows, key_rows, value_rows, grad_rows, allowed, scale_factor
            )
            query_all = lax.dynamic_update_slice_in_dim(
                query_all, query_part.astype(jnp.bfloat16), row_start, 0
            )
            acc_keys = lax.dynamic_update_slice_in_dim(
                acc_keys,
                lax.dynamic_slice_in_dim(acc_keys, key_start, window_rows, 0) + key_part,
                key_start,
                0,
            )
            acc_values = lax.dynamic_update_slice_in_dim(
                acc_values,
                lax.dynamic_slice_in_dim(acc_values, key_start, window_rows, 0) + value_part,
                key_start,
                0,
            )
            return (query_all, acc_keys, acc_values)

        initial = (
            jnp.zeros((group, head_width), jnp.bfloat16),
            jnp.zeros((padded_len, head_width), jnp.float32),
            jnp.zeros((padded_len, head_width), jnp.float32),
        )
        return lax.fori_loop(0, group // block_rows, block_step, initial)

    head_inputs = (
        heads_first(queries, heads_here, head_width),
        heads_first(grads_in, heads_here, head_width),
        heads_first(padded[0], heads_here, head_width),
        heads_first(padded[1], heads_here, head_width),
    )
    query_heads, key_acc, value_acc = lax.map(one_head, head_inputs)
    partials = jnp.stack([key_acc, value_acc])
    own_grads = partials[:, :, group : group + group]
    back_right = from_behind(partials[:, :, group + group :], "seq", 1)
    back_left = from_behind(partials[:, :, :group], "seq", -1)
    own_grads = own_grads.at[:, :, :group].add(back_right)
    own_grads = own_grads.at[:, :, group - group :].add(back_left)
    query_out = heads_last(query_heads)
    key_out = heads_last(own_grads[0]).astype(jnp.bfloat16)
    value_out = heads_last(own_grads[1]).astype(jnp.bfloat16)
    return (
        lax.all_to_all(query_out, "blk", split_axis=0, concat_axis=1, tiled=True),
        lax.all_to_all(key_out, "blk", split_axis=0, concat_axis=1, tiled=True),
        lax.all_to_all(value_out, "blk", split_axis=0, concat_axis=1, tiled=True),
    )


def solution(mesh):
    in_specs = (
        P(("seq", "blk"), None),
        P(("seq", "blk"), None),
        P(("seq", "blk"), None),
        P(("seq", "blk"), None),
        P(),
        P(),
    )
    out_specs = (P(("seq", "blk"), None), P(("seq", "blk"), None), P(("seq", "blk"), None))
    return jax.shard_map(
        per_device, mesh=mesh, in_specs=in_specs, out_specs=out_specs, check_vma=False
    )
```

profile of v0, /device:TPU:18, one launch (start us, length us, event | category | flops | bytes accessed | tf_op | source)
XLA Modules:
  0.0 295.9 jit_solution(5169671486999940543)
XLA Ops:
  2.7 3.5 %all-to-all-start.1 = ((bf16[128,2,1024]{0,2,1:T(8,128)(2,1)}), bf16[128,2,1024]{0,2,1:T(8,128)(2,1)S(1)}, u32[]{:S(2)}, u32[]{:S(2)}) async-start(bf16[128,2,1024]{0,2,1:T(8,128)(2,1)} %bitcast.12), calls=%async_computation.1 | async-start | bytes 1048576 | tf_op jit(solution)/shard_map/all_to_all | solution.py:65
  8.3 6.1 %all-to-all-done.1 = bf16[128,2,1024]{0,2,1:T(8,128)(2,1)S(1)} async-done(((bf16[128,2,1024]{0,2,1:T(8,128)(2,1)}), bf16[128,2,1024]{0,2,1:T(8,128)(2,1)S(1)}, u32[]{:S(2)}, u32[]{:S(2)}) %all-to-all-start.1) | async-done | bytes 524320 | tf_op jit(solution)/shard_map/all_to_all | solution.py:65
  14.4 3.5 %all-to-all-start.2 = ((bf16[128,2,1024]{0,2,1:T(8,128)(2,1)}), bf16[128,2,1024]{0,2,1:T(8,128)(2,1)S(1)}, u32[]{:S(2)}, u32[]{:S(2)}) async-start(bf16[128,2,1024]{0,2,1:T(8,128)(2,1)} %bitcast.15), calls=%async_computation.2 | async-start | bytes 1048576 | tf_op jit(solution)/shard_map/all_to_all | solution.py:66
  18.2 7.1 %all-to-all-done.2 = bf16[128,2,1024]{0,2,1:T(8,128)(2,1)S(1)} async-done(((bf16[128,2,1024]{0,2,1:T(8,128)(2,1)}), bf16[128,2,1024]{0,2,1:T(8,128)(2,1)S(1)}, u32[]{:S(2)}, u32[]{:S(2)}) %all-to-all-start.2) | async-done | bytes 524320 | tf_op jit(solution)/shard_map/all_to_all | solution.py:66
  28.6 2.4 collective-permute-start
  32.0 3.5 %all-to-all-start = ((bf16[128,2,1024]{0,2,1:T(8,128)(2,1)}), bf16[128,2,1024]{0,2,1:T(8,128)(2,1)S(1)}, u32[]{:S(2)}, u32[]{:S(2)}) async-start(bf16[128,2,1024]{0,2,1:T(8,128)(2,1)} %bitcast.9), calls=%async_computation | async-start | bytes 1048576 | tf_op jit(solution)/shard_map/all_to_all | solution.py:64
  36.6 8.1 %all-to-all-done = bf16[128,2,1024]{0,2,1:T(8,128)(2,1)S(1)} async-done(((bf16[128,2,1024]{0,2,1:T(8,128)(2,1)}), bf16[128,2,1024]{0,2,1:T(8,128)(2,1)S(1)}, u32[]{:S(2)}, u32[]{:S(2)}) %all-to-all-start) | async-done | bytes 524320 | tf_op jit(solution)/shard_map/all_to_all | solution.py:64
  44.7 4.2 %all-to-all-start.3 = ((bf16[128,2,1024]{0,2,1:T(8,128)(2,1)}), bf16[128,2,1024]{0,2,1:T(8,128)(2,1)}, u32[]{:S(2)}, u32[]{:S(2)}) async-start(bf16[128,2,1024]{0,2,1:T(8,128)(2,1)} %bitcast.20), calls=%async_computation.3 | async-start | bytes 1048576 | tf_op jit(solution)/shard_map/all_to_all | solution.py:67
  49.1 2.4 copy.53
  53.7 4.2 %all-to-all-done.3 = bf16[128,2,1024]{0,2,1:T(8,128)(2,1)} async-done(((bf16[128,2,1024]{0,2,1:T(8,128)(2,1)}), bf16[128,2,1024]{0,2,1:T(8,128)(2,1)}, u32[]{:S(2)}, u32[]{:S(2)}) %all-to-all-start.3) | async-done | bytes 524320 | tf_op jit(solution)/shard_map/all_to_all | solution.py:67
  57.9 2.4 copy.60
  60.2 2.2 reshape.254
  66.5 2.6 copy.61
  69.1 2.6 copy.58
  71.7 143.9 %while.28 = (s32[]{:T(128)}, bf16[16,256,64]{1,2,0:T(8,128)(2,1)}, f32[16,768,64]{1,2,0:T(8,128)}, f32[16,768,64]{1,2,0:T(8,128)S(1)}, s32[]{:T(128)}, /*index=5...) while((s32[]{:T(128)}, bf16[16,256,64]{1,2,0:T(8,128)(2,1)}, ...), condition=%wide.region_4.5_spmd, body=%wide.region_0.4_spmd.sunk | while | flops 154271200 | bytes 6505753 | solution.py:141
  215.6 4.5 %fusion.38 = (f32[2,16,256,64]{2,3,1,0:T(8,128)}, f32[2,16,256,64]{2,3,1,0:T(8,128)}) fusion(f32[1,16,768,64]{2,3,1,0:T(8,128)} %bitcast.135, f32[1,16,768,64]{2,3,1,0:T(8,128)S(1)} %bitcast.133), kind=kLoop, calls=%fused_computation.56 | loop fusion | flops 1048576 | bytes 10485760 | tf_op jit(solution)/shard_map/stack | solution.py:142
  221.9 3.6 %collective-permute-start.3 = (f32[2,16,256,64]{2,3,1,0:T(8,128)}, f32[2,16,256,64]{2,3,1,0:T(8,128)}, u32[]{:S(2)}, u32[]{:S(2)}) collective-permute-start(f32[2,16,256,64]{2,3,1,0:T(8,128)} %get-tuple-element.346), channel_id=1, source_target_pairs={{2,0},{4,2},{6,4},{8,6},{10,8},{12,10},{14,12},{16,14},{18,16},{20... | collective-permute-start | bytes 6291464 | tf_op jit(solution)/shard_map/ppermute | solution.py:14
  229.6 4.2 %all-to-all-start.4 = ((bf16[2,128,1024]{2,1,0:T(8,128)(2,1)}), bf16[2,128,1024]{2,1,0:T(8,128)(2,1)}, u32[]{:S(2)}, u32[]{:S(2)}) async-start(bf16[2,128,1024]{2,1,0:T(8,128)(2,1)} %copy.65), calls=%async_computation.4 | async-start | bytes 1048576 | tf_op jit(solution)/shard_map/all_to_all | solution.py:152
  233.8 36.4 %collective-permute-done.2 = f32[2,16,256,64]{2,3,1,0:T(8,128)} collective-permute-done((f32[2,16,256,64]{2,3,1,0:T(8,128)}, f32[2,16,256,64]{2,3,1,0:T(8,128)}, u32[]{:S(2)}, u32[]{:S(2)}) %collective-permute-start.2) | collective-permute-done | bytes 2097184 | tf_op jit(solution)/shard_map/ppermute | solution.py:14
  270.2 3.0 %fusion.42 = bf16[2,16,256,64]{2,3,1,0:T(8,128)(2,1)S(1)} fusion(f32[2,16,256,64]{2,3,1,0:T(8,128)} %collective-permute-done.3, f32[2,16,256,64]{2,3,1,0:T(8,128)} %collective-permute-done.2, f32[1,16,768,64]{2,3,1,0:T(8,128)} %bitcast.136, f32[1,16,768,64]{2,3,1,0:T(8,128)S(1)} %bitcast.134), kind=kLoop, calls=%fused_computation.60 | loop fusion | flops 2097152 | bytes 11534336 | tf_op jit(solution)/shard_map/convert.1
  274.5 3.5 %all-to-all-start.6 = ((bf16[2,128,1024]{2,1,0:T(8,128)(2,1)}), bf16[2,128,1024]{2,1,0:T(8,128)(2,1)S(1)}, u32[]{:S(2)}, u32[]{:S(2)}) async-start(bf16[2,128,1024]{2,1,0:T(8,128)(2,1)} %copy.69), calls=%async_computation.6 | async-start | bytes 1048576 | tf_op jit(solution)/shard_map/all_to_all | solution.py:154
  279.2 5.3 %all-to-all-done.6 = bf16[2,128,1024]{2,1,0:T(8,128)(2,1)S(1)} async-done(((bf16[2,128,1024]{2,1,0:T(8,128)(2,1)}), bf16[2,128,1024]{2,1,0:T(8,128)(2,1)S(1)}, u32[]{:S(2)}, u32[]{:S(2)}) %all-to-all-start.6) | async-done | bytes 524320 | tf_op jit(solution)/shard_map/all_to_all | solution.py:154
  284.5 3.5 %all-to-all-start.5 = ((bf16[2,128,1024]{2,1,0:T(8,128)(2,1)}), bf16[2,128,1024]{2,1,0:T(8,128)(2,1)S(1)}, u32[]{:S(2)}, u32[]{:S(2)}) async-start(bf16[2,128,1024]{2,1,0:T(8,128)(2,1)} %copy.67), calls=%async_computation.5 | async-start | bytes 1048576 | tf_op jit(solution)/shard_map/all_to_all | solution.py:153
  291.7 2.9 all-to-all-done.5
  (272 shorter events, 172.6 us)
Async XLA Ops:
  0.6 48.4 %copy-start = (s32[32,2]{0,1:T(2,128)S(1)}, s32[32,2]{0,1:T(2,128)}, u32[]{:S(2)}) copy-start(s32[32,2]{0,1:T(2,128)} %param.20) | copy-start | bytes 772
  2.7 11.7 %all-to-all-start.1 = ((bf16[128,2,1024]{0,2,1:T(8,128)(2,1)}), bf16[128,2,1024]{0,2,1:T(8,128)(2,1)S(1)}, u32[]{:S(2)}, u32[]{:S(2)}) async-start(bf16[128,2,1024]{0,2,1:T(8,128)(2,1)} %bitcast.12), calls=%async_computation.1 | async-start | bytes 1048576 | tf_op jit(solution)/shard_map/all_to_all | solution.py:65
  6.2 24.8 %copy-start.4 = (bf16[128,2048]{1,0:T(8,128)(2,1)S(1)}, bf16[128,2048]{1,0:T(8,128)(2,1)}, u32[]{:S(2)}) copy-start(bf16[128,2048]{1,0:T(8,128)(2,1)} %param.16) | copy-start | bytes 1572868
  14.4 10.9 %all-to-all-start.2 = ((bf16[128,2,1024]{0,2,1:T(8,128)(2,1)}), bf16[128,2,1024]{0,2,1:T(8,128)(2,1)S(1)}, u32[]{:S(2)}, u32[]{:S(2)}) async-start(bf16[128,2,1024]{0,2,1:T(8,128)(2,1)} %bitcast.15), calls=%async_computation.2 | async-start | bytes 1048576 | tf_op jit(solution)/shard_map/all_to_all | solution.py:66
  17.9 17.6 %copy-start.5 = (bf16[128,2048]{1,0:T(8,128)(2,1)S(1)}, bf16[128,2048]{1,0:T(8,128)(2,1)}, u32[]{:S(2)}) copy-start(bf16[128,2048]{1,0:T(8,128)(2,1)} %param.19) | copy-start | bytes 1572868
  18.2 18.4 %copy-start.1 = (bf16[2,128,1024]{2,1,0:T(8,128)(2,1)}, bf16[2,128,1024]{2,1,0:T(8,128)(2,1)S(1)}, u32[]{:S(2)}) copy-start(bf16[2,128,1024]{2,1,0:T(8,128)(2,1)S(1)} %copy.55) | copy-start | bytes 1572868
  25.5 19.2 %copy-start.2 = (bf16[2,128,1024]{2,1,0:T(8,128)(2,1)}, bf16[2,128,1024]{2,1,0:T(8,128)(2,1)S(1)}, u32[]{:S(2)}) copy-start(bf16[2,128,1024]{2,1,0:T(8,128)(2,1)S(1)} %copy.57) | copy-start | bytes 1572868
  25.5 23.4 %copy-start.6 = (s32[32]{0:T(128)S(1)}, s32[32]{0:T(128)}, u32[]{:S(2)}) copy-start(s32[32]{0:T(128)} %param.21) | copy-start | bytes 388
  26.7 35.8 %collective-permute-start.1 = (bf16[2,256,1024]{2,1,0:T(8,128)(2,1)}, bf16[2,256,1024]{2,1,0:T(8,128)(2,1)}, u32[]{:S(2)}, u32[]{:S(2)}) collective-permute-start(bf16[2,256,1024]{2,1,0:T(8,128)(2,1)} %pad_maximum_fusion.2), channel_id=1, source_target_pairs={{2,0},{4,2},{6,4},{8,6},{10,8},{12,10},{14,12},{16,14},{18,16},{20... | collective-permute-start | bytes 3145736 | tf_op jit(solution)/shard_map/ppermute | solution.py:14
  28.6 33.8 %collective-permute-start = (bf16[2,256,1024]{2,1,0:T(8,128)(2,1)}, bf16[2,256,1024]{2,1,0:T(8,128)(2,1)}, u32[]{:S(2)}, u32[]{:S(2)}) collective-permute-start(bf16[2,256,1024]{2,1,0:T(8,128)(2,1)} %pad_maximum_fusion.2), channel_id=1, source_target_pairs={{0,2},{2,4},{4,6},{6,8},{8,10},{10,12},{12,14},{14,16},{16,18},{18... | collective-permute-start | bytes 3145736 | tf_op jit(solution)/shard_map/ppermute | solution.py:14
  32.0 12.7 %all-to-all-start = ((bf16[128,2,1024]{0,2,1:T(8,128)(2,1)}), bf16[128,2,1024]{0,2,1:T(8,128)(2,1)S(1)}, u32[]{:S(2)}, u32[]{:S(2)}) async-start(bf16[128,2,1024]{0,2,1:T(8,128)(2,1)} %bitcast.9), calls=%async_computation | async-start | bytes 1048576 | tf_op jit(solution)/shard_map/all_to_all | solution.py:64
  44.7 4.2 %copy-start.3 = (bf16[128,2,1024]{0,2,1:T(8,128)(2,1)}, bf16[128,2,1024]{0,2,1:T(8,128)(2,1)S(1)}, u32[]{:S(2)}) copy-start(bf16[128,2,1024]{0,2,1:T(8,128)(2,1)S(1)} %all-to-all-done) | copy-start | bytes 1572868
  44.7 13.1 %all-to-all-start.3 = ((bf16[128,2,1024]{0,2,1:T(8,128)(2,1)}), bf16[128,2,1024]{0,2,1:T(8,128)(2,1)}, u32[]{:S(2)}, u32[]{:S(2)}) async-start(bf16[128,2,1024]{0,2,1:T(8,128)(2,1)} %bitcast.20), calls=%async_computation.3 | async-start | bytes 1048576 | tf_op jit(solution)/shard_map/all_to_all | solution.py:67
  220.0 50.1 %collective-permute-start.2 = (f32[2,16,256,64]{2,3,1,0:T(8,128)}, f32[2,16,256,64]{2,3,1,0:T(8,128)}, u32[]{:S(2)}, u32[]{:S(2)}) collective-permute-start(f32[2,16,256,64]{2,3,1,0:T(8,128)} %get-tuple-element.345), channel_id=1, source_target_pairs={{0,2},{2,4},{4,6},{6,8},{8,10},{10,12},{12,14},{14,16},{16,18},{18... | collective-permute-start | bytes 6291464 | tf_op jit(solution)/shard_map/ppermute | solution.py:14
  221.9 48.2 %collective-permute-start.3 = (f32[2,16,256,64]{2,3,1,0:T(8,128)}, f32[2,16,256,64]{2,3,1,0:T(8,128)}, u32[]{:S(2)}, u32[]{:S(2)}) collective-permute-start(f32[2,16,256,64]{2,3,1,0:T(8,128)} %get-tuple-element.346), channel_id=1, source_target_pairs={{2,0},{4,2},{6,4},{8,6},{10,8},{12,10},{14,12},{16,14},{18,16},{20... | collective-permute-start | bytes 6291464 | tf_op jit(solution)/shard_map/ppermute | solution.py:14
  229.6 44.9 %all-to-all-start.4 = ((bf16[2,128,1024]{2,1,0:T(8,128)(2,1)}), bf16[2,128,1024]{2,1,0:T(8,128)(2,1)}, u32[]{:S(2)}, u32[]{:S(2)}) async-start(bf16[2,128,1024]{2,1,0:T(8,128)(2,1)} %copy.65), calls=%async_computation.4 | async-start | bytes 1048576 | tf_op jit(solution)/shard_map/all_to_all | solution.py:152
  274.5 10.1 %all-to-all-start.6 = ((bf16[2,128,1024]{2,1,0:T(8,128)(2,1)}), bf16[2,128,1024]{2,1,0:T(8,128)(2,1)S(1)}, u32[]{:S(2)}, u32[]{:S(2)}) async-start(bf16[2,128,1024]{2,1,0:T(8,128)(2,1)} %copy.69), calls=%async_computation.6 | async-start | bytes 1048576 | tf_op jit(solution)/shard_map/all_to_all | solution.py:154
  284.5 10.1 %all-to-all-start.5 = ((bf16[2,128,1024]{2,1,0:T(8,128)(2,1)}), bf16[2,128,1024]{2,1,0:T(8,128)(2,1)S(1)}, u32[]{:S(2)}, u32[]{:S(2)}) async-start(bf16[2,128,1024]{2,1,0:T(8,128)(2,1)} %copy.67), calls=%async_computation.5 | async-start | bytes 1048576 | tf_op jit(solution)/shard_map/all_to_all | solution.py:153
where the time goes:
time: 301 us; the launch traced here: 296 us
  matrix products  135 us (45%)
  waiting for transfers between devices  70.2 us (23%)
  local copies, waits for them, and re-layouts  36.8 us (12%)
  starting transfers between devices  35.7 us (12%)
  other arithmetic  17 us (6%)
    ppermute x4, waiting for transfers between devices, from_behind(): return lax.ppermute(block, axis, route)  36.4 us
    dot_general x16, matrix products, block_grad(): jnp.dot(dscores, key_rows, preferred_element_type=jnp.float32)  28.6 us
    dot_general x16, matrix products, block_grad(): jnp.dot(dscores.T, query_rows, preferred_element_type=jnp.float32)  26.5 us
    dot_general x16, matrix products, block_grad(): attn_out = jnp.dot(probs_b, value_rows, preferred_element_type=jnp.float32)  21.1 us
    dot_general x16, matrix products, block_grad(): jnp.dot(query_rows, key_rows.T, preferred_element_type=jnp.float32)  21 us
    dot_general x16, matrix products, block_grad(): jnp.dot(grad_rows, value_rows.T, preferred_element_type=jnp.float32)  19.8 us
    dot_general x16, matrix products, block_grad(): jnp.dot(probs_b.T, grad_rows, preferred_element_type=jnp.float32)  17.7 us
    ppermute x4, starting transfers between devices, from_behind(): return lax.ppermute(block, axis, route)  9.87 us
  transfers between devices with their start and end apart: 11, of which 7 were waited for; matrix products, arithmetic and copies ran while one was open for 8% of the time, Pallas kernels for 0%

commit v1 on v0

v1 whole, which is shorter than its diff:
```python
import functools

import jax
import jax.numpy as jnp
from jax import lax
from jax.experimental import pallas as pl
from jax.experimental.pallas import tpu as pltpu
from jax.sharding import PartitionSpec as P

HEAD_DIM = 64
TILE = 128
REACH = 2
RIM = REACH * TILE
WINDOW = 2 * REACH + 1
PAIR = 2 * HEAD_DIM
WIDTH = 128
FINISH_LAG = 2
NEG = -1e30
MESH = pl.DeviceIdType.MESH
F32 = jnp.float32
BF16 = jnp.bfloat16


def stack_heads(rows, scale):
    lane = lax.broadcasted_iota(jnp.int32, rows.shape, 1)
    zero = jnp.zeros_like(rows)
    rows = rows * jnp.asarray(scale, rows.dtype)
    return jnp.concatenate(
        [jnp.where(lane < HEAD_DIM, rows, zero), jnp.where(lane >= HEAD_DIM, rows, zero)], axis=0
    )


def unit_grad(query, grad, keys, values, allow):
    contract_last = (((1,), (1,)), ((), ()))
    contract_first = (((0,), (0,)), ((), ()))
    scale = float(HEAD_DIM) ** (-0.5)
    query_two = stack_heads(query, scale)
    grad_two = stack_heads(grad, 1.0)
    scores = lax.dot_general(keys, query_two, contract_last, preferred_element_type=F32)
    dprobs = lax.dot_general(values, grad_two, contract_last, preferred_element_type=F32)
    tiles = [scores[j * TILE : (j + 1) * TILE] for j in range(WINDOW)]
    peak = None
    for ok, tile in zip(allow, tiles):
        top = jnp.where(ok, jnp.max(tile, axis=0, keepdims=True), NEG)
        peak = top if peak is None else jnp.maximum(peak, top)
    raw = [jnp.exp(tile - jnp.where(ok, peak, -NEG)) for ok, tile in zip(allow, tiles)]
    raw = jnp.concatenate(raw, axis=0)
    probs = raw * (1.0 / jnp.sum(raw, axis=0, keepdims=True))
    delta = jnp.sum(probs * dprobs, axis=0, keepdims=True)
    dscores = (probs * (dprobs - delta)).astype(BF16)
    value_part = jnp.dot(probs.astype(BF16), grad_two, preferred_element_type=F32)
    key_part = jnp.dot(dscores, query_two, preferred_element_type=F32)
    both = lax.dot_general(keys, dscores, contract_first, preferred_element_type=F32)
    row = lax.broadcasted_iota(jnp.int32, (PAIR, TILE), 0)
    query_part = jnp.where(row < HEAD_DIM, both[:, :TILE], both[:, TILE:])
    return (query_part.T * scale).astype(BF16), key_part, value_part


def kernel(
    seqs, group, feats,
    q_in, k_in, v_in, g_in, near, motion,
    dq_out, dk_out, dv_out,
    qg, kv, dq, acc, part_out, part_in, done,
    in_send, in_recv, halo_send, halo_recv, part_send, part_recv, out_send, out_recv,
):
    seq, blk = lax.axis_index("seq"), lax.axis_index("blk")
    chunks = feats // WIDTH
    own = group * TILE
    has_left, has_right = seq > 0, seq < seqs - 1
    left, right = (seq - 1, blk), (seq + 1, blk)
    tiles_all = near.shape[0]
    inputs = (k_in, v_in, q_in, g_in)
    outputs = (dq_out, dk_out, dv_out)

    barrier = pltpu.get_barrier_semaphore()
    for r in range(1, group):
        pl.semaphore_signal(barrier, inc=1, device_id=(seq, lax.rem(blk + r, group)), device_id_type=MESH)

    @pl.when(has_left)
    def _():
        pl.semaphore_signal(barrier, inc=1, device_id=left, device_id_type=MESH)

    @pl.when(has_right)
    def _():
        pl.semaphore_signal(barrier, inc=1, device_id=right, device_id_type=MESH)

    pl.semaphore_wait(barrier, group - 1 + has_left.astype(jnp.int32) + has_right.astype(jnp.int32))

    def columns(owner, c):
        return pl.ds(pl.multiple_of(owner * feats + c * WIDTH, 128), WIDTH)

    def tile_rows(tile, first=0):
        return pl.ds(pl.multiple_of(first + tile * TILE, TILE), TILE)

    def in_place(a, c, tile):
        if a < 2:
            return kv.at[c, a, tile_rows(tile, RIM)]
        return qg.at[c, a - 2, tile_rows(tile)]

    def in_local(a, c):
        return pltpu.make_async_copy(inputs[a].at[:, columns(blk, c)], in_place(a, c, blk), in_recv.at[c, a, 0])

    def in_remote(a, c, r):
        peer = lax.rem(blk + r, group)
        return pltpu.make_async_remote_copy(
            src_ref=inputs[a].at[:, columns(peer, c)],
            dst_ref=in_place(a, c, blk),
            send_sem=in_send.at[c, a, r - 1],
            recv_sem=in_recv.at[c, a, r],
            device_id=(seq, peer),
            device_id_type=MESH,
        )

    def halo(c, side):
        source = RIM if side == 0 else own
        target = RIM + own if side == 0 else 0
        return pltpu.make_async_remote_copy(
            src_ref=kv.at[c, :, pl.ds(source, RIM)],
            dst_ref=kv.at[c, :, pl.ds(target, RIM)],
            send_sem=halo_send.at[c, side],
            recv_sem=halo_recv.at[c, side],
            device_id=left if side == 0 else right,
            device_id_type=MESH,
        )

    def partial(c, side):
        return pltpu.make_async_remote_copy(
            src_ref=part_out.at[c, side],
            dst_ref=part_in.at[c, side],
            send_sem=part_send.at[c, side],
            recv_sem=part_recv.at[c, side],
            device_id=left if side == 0 else right,
            device_id_type=MESH,
        )

    def out_source(a, c, tile):
        if a == 0:
            return dq.at[c, tile_rows(tile)]
        return done.at[c, a - 1, tile_rows(tile)]

    def out_local(a, c):
        return pltpu.make_async_copy(
            out_source(a, c, blk), outputs[a].at[:, columns(blk, c)], out_recv.at[c, a, 0]
        )

    def out_remote(a, c, r):
        peer = lax.rem(blk + r, group)
        return pltpu.make_async_remote_copy(
            src_ref=out_source(a, c, peer),
            dst_ref=outputs[a].at[:, columns(blk, c)],
            send_sem=out_send.at[c, a, r - 1],
            recv_sem=out_recv.at[c, a, r],
            device_id=(seq, peer),
            device_id_type=MESH,
        )

    def sides(action):
        pl.when(has_left)(lambda: action(0))
        pl.when(has_right)(lambda: action(1))

    def arrivals(action):
        pl.when(has_right)(lambda: action(0))
        pl.when(has_left)(lambda: action(1))

    def send_in(c, _):
        for a in range(4):
            for r in range(1, group):
                in_remote(a, c, r).start()
            in_local(a, c).start()
        return 0

    lax.fori_loop(0, chunks, send_in, 0)

    @pl.when(jnp.logical_not(has_left))
    def _():
        kv[:, :, 0:RIM, :] = jnp.zeros((chunks, 2, RIM, WIDTH), BF16)
        part_in[:, 1] = jnp.zeros((chunks, 2, RIM, WIDTH), BF16)

    @pl.when(jnp.logical_not(has_right))
    def _():
        kv[:, :, RIM + own :, :] = jnp.zeros((chunks, 2, RIM, WIDTH), BF16)
        part_in[:, 0] = jnp.zeros((chunks, 2, RIM, WIDTH), BF16)

    allow = []
    for tile in range(group):
        at = seq * group + tile
        far = motion[at] >= 2
        oks = [far & (at >= 2), (near[at, 0] == 1) & (at >= 1), None,
               (near[at, 1] == 1) & (at + 1 < tiles_all), far & (at + 2 < tiles_all)]
        oks[2] = at >= 0
        allow.append(oks)

    def wait_in(c, arrays):
        for a in arrays:
            in_local(a, c).wait()
            for r in range(1, group):
                in_remote(a, c, r).wait_recv()

    def send_halo(c):
        wait_in(c, (0, 1))
        sides(lambda side: halo(c, side).start())

    def compute(c):
        wait_in(c, (2, 3))
        arrivals(lambda side: halo(c, side).wait_recv())
        for p in range(WIDTH // PAIR):
            cols = slice(p * PAIR, (p + 1) * PAIR)
            for tile in range(group):
                rows = slice(tile * TILE, (tile + 1) * TILE)
                span = slice(tile * TILE, (tile + WINDOW) * TILE)
                query_part, key_part, value_part = unit_grad(
                    qg[c, 0, rows, cols], qg[c, 1, rows, cols], kv[c, 0, span, cols], kv[c, 1, span, cols],
                    allow[tile],
                )
                dq[c, rows, cols] = query_part
                for a, part in ((0, key_part), (1, value_part)):
                    if tile == 0:
                        acc[c, a, span, cols] = part
                    else:
                        old = slice(tile * TILE, (tile + WINDOW - 1) * TILE)
                        new = slice((tile + WINDOW - 1) * TILE, (tile + WINDOW) * TILE)
                        acc[c, a, old, cols] = acc[c, a, old, cols] + part[: (WINDOW - 1) * TILE]
                        acc[c, a, new, cols] = part[(WINDOW - 1) * TILE :]
        part_out[c, 0] = acc[c, :, 0:RIM].astype(BF16)
        part_out[c, 1] = acc[c, :, RIM + own :].astype(BF16)
        sides(lambda side: partial(c, side).start())
        send_out(c, (0,))

    def send_out(c, arrays):
        for a in arrays:
            for r in range(1, group):
                out_remote(a, c, r).start()
            out_local(a, c).start()

    def finish(c):
        arrivals(lambda side: partial(c, side).wait_recv())
        total = acc[c, :, RIM : RIM + own]
        first = part_in[c, 1].astype(F32)
        last = part_in[c, 0].astype(F32)
        if group == REACH:
            done[c] = (total + first + last).astype(BF16)
        else:
            done[c, :, 0 : own - RIM] = total[:, 0 : own - RIM].astype(BF16)
            done[c, :, 0:RIM] = (total[:, 0:RIM] + first).astype(BF16)
            tail = total[:, own - RIM :] + last
            if own < 2 * RIM:
                tail = tail + jnp.pad(first, ((0, 0), (0, own - RIM), (0, 0)))[:, own - RIM :]
            done[c, :, own - RIM :] = tail.astype(BF16)
        send_out(c, (1, 2))

    send_halo(0)
    if chunks > 1:
        send_halo(1)

    def step(c, _):
        pl.when(c + 2 < chunks)(lambda: send_halo(c + 2))
        compute(c)
        pl.when(c >= FINISH_LAG)(lambda: finish(c - FINISH_LAG))
        return 0

    lax.fori_loop(0, chunks, step, 0)
    lax.fori_loop(max(chunks - FINISH_LAG, 0), chunks, lambda c, _: (finish(c), 0)[1], 0)

    def drain(c, _):
        for a in range(4):
            for r in range(1, group):
                in_remote(a, c, r).wait_send()
        sides(lambda side: halo(c, side).wait_send())
        sides(lambda side: partial(c, side).wait_send())
        for a in range(3):
            out_local(a, c).wait()
            for r in range(1, group):
                out_remote(a, c, r).wait_send()
                out_remote(a, c, r).wait_recv()
        return 0

    lax.fori_loop(0, chunks, drain, 0)


def per_device(seqs, group, query_states, key_states, value_states, output_grad, near_mask, motion_count):
    rows, width = query_states.shape
    assert rows == TILE
    feats = width // group
    chunks = feats // WIDTH
    own = group * TILE
    window = own + 2 * RIM
    result = jax.ShapeDtypeStruct((rows, width), BF16)
    dma = pltpu.SemaphoreType.DMA
    return pl.pallas_call(
        functools.partial(kernel, seqs, group, feats),
        out_shape=(result, result, result),
        in_specs=[pl.BlockSpec(memory_space=pl.ANY)] * 4 + [pl.BlockSpec(memory_space=pltpu.SMEM)] * 2,
        out_specs=[pl.BlockSpec(memory_space=pl.ANY)] * 3,
        scratch_shapes=[
            pltpu.VMEM((chunks, 2, own, WIDTH), BF16),
            pltpu.VMEM((chunks, 2, window, WIDTH), BF16),
            pltpu.VMEM((chunks, own, WIDTH), BF16),
            pltpu.VMEM((chunks, 2, window, WIDTH), F32),
            pltpu.VMEM((chunks, 2, 2, RIM, WIDTH), BF16),
            pltpu.VMEM((chunks, 2, 2, RIM, WIDTH), BF16),
            pltpu.VMEM((chunks, 2, own, WIDTH), BF16),
            dma((chunks, 4, group - 1)),
            dma((chunks, 4, group)),
            dma((chunks, 2)),
            dma((chunks, 2)),
            dma((chunks, 2)),
            dma((chunks, 2)),
            dma((chunks, 3, group - 1)),
            dma((chunks, 3, group)),
        ],
        compiler_params=pltpu.CompilerParams(
            collective_id=0, has_side_effects=True, vmem_limit_bytes=48 * 1024 * 1024
        ),
    )(query_states, key_states, value_states, output_grad, near_mask, motion_count)


def solution(mesh):
    tokens = P(("seq", "blk"), None)
    return jax.shard_map(
        functools.partial(per_device, mesh.shape["seq"], mesh.shape["blk"]),
        mesh=mesh,
        in_specs=(tokens, tokens, tokens, tokens, P(), P()),
        out_specs=(tokens, tokens, tokens),
        check_vma=False,
    )
```

time: 301 us -> 68.5 us (0.23)
  the two profiles are of different devices: /device:TPU:18 before, /device:TPU:1 now
where the time goes in v1:
time: 68.5 us; the launch traced here: 68.2 us
  Pallas kernels  60.2 us (88%)
  local copies, waits for them, and re-layouts  7.32 us (11%)
    pallas_call x1, Pallas kernels, per_device(): pl.pallas_call(functools.partial(kernel, seqs, group, feats), out_shape=(...  60.2 us
    unnamed x14, local copies, waits for them, and re-layouts  7.32 us

profile of v1, /device:TPU:1, one launch (start us, length us, event | category | flops | bytes accessed | tf_op | source)
XLA Modules:
  0.0 68.2 jit_solution(5552611857000703694)
XLA Ops:
  0.6 0.0 copy-start.4
  0.6 0.8 %copy.9.near = s32[32,2]{1,0:T(8,128)S(1)} copy(s32[32,2]{0,1:T(2,128)} %param.10) | data formatting | bytes 512 | tf_op args[4]
  1.4 0.0 copy-done.4
  1.4 0.0 copy-start
  1.4 1.0 %copy-done = bf16[128,2048]{1,0:T(8,128)(2,1)S(1)} copy-done((bf16[128,2048]{1,0:T(8,128)(2,1)S(1)}, bf16[128,2048]{1,0:T(8,128)(2,1)}, u32[]{:S(2)}) %copy-start) | copy-done | bytes 524312
  2.5 0.0 copy-start.1
  2.5 1.0 %copy-done.1 = bf16[128,2048]{1,0:T(8,128)(2,1)S(1)} copy-done((bf16[128,2048]{1,0:T(8,128)(2,1)S(1)}, bf16[128,2048]{1,0:T(8,128)(2,1)}, u32[]{:S(2)}) %copy-start.1) | copy-done | bytes 524312
  3.5 0.0 copy-start.2
  3.5 1.0 %copy-done.2 = bf16[128,2048]{1,0:T(8,128)(2,1)S(1)} copy-done((bf16[128,2048]{1,0:T(8,128)(2,1)S(1)}, bf16[128,2048]{1,0:T(8,128)(2,1)}, u32[]{:S(2)}) %copy-start.2) | copy-done | bytes 524312
  4.5 0.0 copy-start.3
  4.5 1.0 %copy-done.3 = bf16[128,2048]{1,0:T(8,128)(2,1)S(1)} copy-done((bf16[128,2048]{1,0:T(8,128)(2,1)S(1)}, bf16[128,2048]{1,0:T(8,128)(2,1)}, u32[]{:S(2)}) %copy-start.3) | copy-done | bytes 524312
  5.6 60.2 %shard_map.85 = (bf16[128,2048]{1,0:T(8,128)(2,1)S(1)}, bf16[128,2048]{1,0:T(8,128)(2,1)S(1)}, bf16[128,2048]{1,0:T(8,128)(2,1)S(1)}) custom-call(bf16[128,2048]{1,0:T(8,128)(2,1)S(1)} %copy-done, bf16[128,2048]{1,0:T(8,128)(2,1)S(1)} %copy-done.1, bf16[128,2048]{1,0:T(8,128)(2,1)S(1)} %copy-done.2, bf16[128,2048]{1,0:T(8,128)(2,1)S(1)} %copy-done.3, ...), custom_call_target="tpu_custom_call" | custom-call | tf_op jit(solution)/shard_map/pallas_call | solution.py:289
  65.8 0.8 %copy.13 = bf16[128,2048]{1,0:T(8,128)(2,1)} copy(bf16[128,2048]{1,0:T(8,128)(2,1)S(1)} %get-tuple-element.6) | data formatting | bytes 1048576
  66.6 0.8 %copy.14 = bf16[128,2048]{1,0:T(8,128)(2,1)} copy(bf16[128,2048]{1,0:T(8,128)(2,1)S(1)} %get-tuple-element.7) | data formatting | bytes 1048576
  67.4 0.8 %copy.15 = bf16[128,2048]{1,0:T(8,128)(2,1)} copy(bf16[128,2048]{1,0:T(8,128)(2,1)S(1)} %get-tuple-element.8) | data formatting | bytes 1048576
Async XLA Ops:
  0.6 0.8 %copy-start.4 = (s32[32]{0:T(128)S(1)}, s32[32]{0:T(128)}, u32[]{:S(2)}) copy-start(s32[32]{0:T(128)} %motion.1) | copy-start | bytes 388
  1.4 1.0 %copy-start = (bf16[128,2048]{1,0:T(8,128)(2,1)S(1)}, bf16[128,2048]{1,0:T(8,128)(2,1)}, u32[]{:S(2)}) copy-start(bf16[128,2048]{1,0:T(8,128)(2,1)} %q_in.1) | copy-start | bytes 1572868
  2.5 1.0 %copy-start.1 = (bf16[128,2048]{1,0:T(8,128)(2,1)S(1)}, bf16[128,2048]{1,0:T(8,128)(2,1)}, u32[]{:S(2)}) copy-start(bf16[128,2048]{1,0:T(8,128)(2,1)} %k_in.1) | copy-start | bytes 1572868
  3.5 1.0 %copy-start.2 = (bf16[128,2048]{1,0:T(8,128)(2,1)S(1)}, bf16[128,2048]{1,0:T(8,128)(2,1)}, u32[]{:S(2)}) copy-start(bf16[128,2048]{1,0:T(8,128)(2,1)} %v_in.1) | copy-start | bytes 1572868
  4.5 1.0 %copy-start.3 = (bf16[128,2048]{1,0:T(8,128)(2,1)S(1)}, bf16[128,2048]{1,0:T(8,128)(2,1)}, u32[]{:S(2)}) copy-start(bf16[128,2048]{1,0:T(8,128)(2,1)} %g_in.1) | copy-start | bytes 1572868

commit v2 on v1

--- a/solution.py
+++ b/solution.py
@@ -13,7 +13,7 @@
 RIM = REACH * TILE
 WINDOW = 2 * REACH + 1
 PAIR = 2 * HEAD_DIM
-WIDTH = 128
+WIDTH = 256
 FINISH_LAG = 2
 NEG = -1e30
 MESH = pl.DeviceIdType.MESH

time: 68.5 us -> 67.1 us (0.980)
  the two profiles are of different devices: /device:TPU:1 before, /device:TPU:18 now
where the time goes in v2:
time: 67.1 us; the launch traced here: 66 us
  Pallas kernels  58.1 us (87%)
  local copies, waits for them, and re-layouts  7.32 us (11%)
    pallas_call x1, Pallas kernels, per_device(): pl.pallas_call(functools.partial(kernel, seqs, group, feats), out_shape=(...  58.1 us
    unnamed x14, local copies, waits for them, and re-layouts  7.32 us

profile of v2, /device:TPU:18, one launch (start us, length us, event | category | flops | bytes accessed | tf_op | source)
XLA Modules:
  0.0 66.0 jit_solution(3505337653708738427)
XLA Ops:
  0.6 0.0 copy-start.4
  0.6 0.8 %copy.9.near = s32[32,2]{1,0:T(8,128)S(1)} copy(s32[32,2]{0,1:T(2,128)} %param.10) | data formatting | bytes 512 | tf_op args[4]
  1.4 0.0 copy-done.4
  1.4 0.0 copy-start
  1.4 1.0 %copy-done = bf16[128,2048]{1,0:T(8,128)(2,1)S(1)} copy-done((bf16[128,2048]{1,0:T(8,128)(2,1)S(1)}, bf16[128,2048]{1,0:T(8,128)(2,1)}, u32[]{:S(2)}) %copy-start) | copy-done | bytes 524312
  2.5 0.0 copy-start.1
  2.5 1.0 %copy-done.1 = bf16[128,2048]{1,0:T(8,128)(2,1)S(1)} copy-done((bf16[128,2048]{1,0:T(8,128)(2,1)S(1)}, bf16[128,2048]{1,0:T(8,128)(2,1)}, u32[]{:S(2)}) %copy-start.1) | copy-done | bytes 524312
  3.5 0.0 copy-start.2
  3.5 1.0 %copy-done.2 = bf16[128,2048]{1,0:T(8,128)(2,1)S(1)} copy-done((bf16[128,2048]{1,0:T(8,128)(2,1)S(1)}, bf16[128,2048]{1,0:T(8,128)(2,1)}, u32[]{:S(2)}) %copy-start.2) | copy-done | bytes 524312
  4.5 0.0 copy-start.3
  4.5 1.0 %copy-done.3 = bf16[128,2048]{1,0:T(8,128)(2,1)S(1)} copy-done((bf16[128,2048]{1,0:T(8,128)(2,1)S(1)}, bf16[128,2048]{1,0:T(8,128)(2,1)}, u32[]{:S(2)}) %copy-start.3) | copy-done | bytes 524312
  5.6 58.1 %shard_map.85 = (bf16[128,2048]{1,0:T(8,128)(2,1)S(1)}, bf16[128,2048]{1,0:T(8,128)(2,1)S(1)}, bf16[128,2048]{1,0:T(8,128)(2,1)S(1)}) custom-call(bf16[128,2048]{1,0:T(8,128)(2,1)S(1)} %copy-done, bf16[128,2048]{1,0:T(8,128)(2,1)S(1)} %copy-done.1, bf16[128,2048]{1,0:T(8,128)(2,1)S(1)} %copy-done.2, bf16[128,2048]{1,0:T(8,128)(2,1)S(1)} %copy-done.3, ...), custom_call_target="tpu_custom_call" | custom-call | tf_op jit(solution)/shard_map/pallas_call | solution.py:289
  63.7 0.8 %copy.13 = bf16[128,2048]{1,0:T(8,128)(2,1)} copy(bf16[128,2048]{1,0:T(8,128)(2,1)S(1)} %get-tuple-element.6) | data formatting | bytes 1048576
  64.5 0.8 %copy.14 = bf16[128,2048]{1,0:T(8,128)(2,1)} copy(bf16[128,2048]{1,0:T(8,128)(2,1)S(1)} %get-tuple-element.7) | data formatting | bytes 1048576
  65.3 0.8 %copy.15 = bf16[128,2048]{1,0:T(8,128)(2,1)} copy(bf16[128,2048]{1,0:T(8,128)(2,1)S(1)} %get-tuple-element.8) | data formatting | bytes 1048576
Async XLA Ops:
  0.6 0.8 %copy-start.4 = (s32[32]{0:T(128)S(1)}, s32[32]{0:T(128)}, u32[]{:S(2)}) copy-start(s32[32]{0:T(128)} %motion.1) | copy-start | bytes 388
  1.4 1.0 %copy-start = (bf16[128,2048]{1,0:T(8,128)(2,1)S(1)}, bf16[128,2048]{1,0:T(8,128)(2,1)}, u32[]{:S(2)}) copy-start(bf16[128,2048]{1,0:T(8,128)(2,1)} %q_in.1) | copy-start | bytes 1572868
  2.5 1.0 %copy-start.1 = (bf16[128,2048]{1,0:T(8,128)(2,1)S(1)}, bf16[128,2048]{1,0:T(8,128)(2,1)}, u32[]{:S(2)}) copy-start(bf16[128,2048]{1,0:T(8,128)(2,1)} %k_in.1) | copy-start | bytes 1572868
  3.5 1.0 %copy-start.2 = (bf16[128,2048]{1,0:T(8,128)(2,1)S(1)}, bf16[128,2048]{1,0:T(8,128)(2,1)}, u32[]{:S(2)}) copy-start(bf16[128,2048]{1,0:T(8,128)(2,1)} %v_in.1) | copy-start | bytes 1572868
  4.5 1.0 %copy-start.3 = (bf16[128,2048]{1,0:T(8,128)(2,1)S(1)}, bf16[128,2048]{1,0:T(8,128)(2,1)}, u32[]{:S(2)}) copy-start(bf16[128,2048]{1,0:T(8,128)(2,1)} %g_in.1) | copy-start | bytes 1572868
